TPU v7x, 512 devices: a whole 4x4x16 slice. The times are simulated.
512 devices in a mesh: build: 16 (over z), gx: 4 (over y), gy: 8 (over x, core).
Axes of the slice: x: 4, y: 4, z: 16, core: 2. Of those that a mesh axis runs over, the one named last changes fastest.
Arguments:
- design: float32 [64, 256, 2048], P('build', 'gx', 'gy'), may hold values from 0 to 1
- cotangent: float32 [64, 256, 2048], P('build', 'gx', 'gy'), may hold values from -6 to 6
Outputs:
- printed: float32 [64, 256, 2048], P('build', 'gx', 'gy')
- gradient: float32 [64, 256, 2048], P('build', 'gx', 'gy')
All inputs are finite; a program needn't handle non-finite values.
Results may differ from a plain program's by a relative error of at most 0.00016.
Values sent between devices are 32-bit elements; how exact they have to be, the bound alone decides.
A program may use at most 64 MiB of HBM per device.

v0:
```python
import jax
import jax.numpy as jnp
from jax import lax
from jax.sharding import PartitionSpec as P

SHARPNESS = 40.0
SOFTNESS = 0.0001
SOFT_ROOT = 0.01


def extended(shard, sides, width):
    for axis, dim in sides:
        size, length = (lax.axis_size(axis), shard.shape[dim])
        up = [(i, (i + 1) % size) for i in range(size - 1)]
        down = [(j, i) for i, j in up]
        last = lax.slice_in_dim(shard, length - width, length, axis=dim)
        initial = lax.slice_in_dim(shard, 0, width, axis=dim)
        before = lax.ppermute(last, axis, up)
        after = lax.ppermute(initial, axis, down)
        shard = jnp.concatenate([before, shard, after], axis=dim)
    return shard


def shifted(value, axis, steps):
    count = lax.axis_size(axis)
    initial, last = (max(0, -steps), min(count, count - steps))
    return lax.ppermute(value, axis, [(source, source + steps) for source in range(initial, last)])


def shifted_sum(values):
    padded = jnp.pad(values, 1)
    return (
        padded[1:-1, 1:-1]
        + padded[:-2, 1:-1]
        + padded[2:, 1:-1]
        + padded[1:-1, :-2]
        + padded[1:-1, 2:]
    )


def widen_deep(values, width):
    return extended(values, (("gx", 1), ("gy", 2)), width)


def extend(values, width):
    return extended(values, (("gx", 0), ("gy", 1)), width)


def block_place(block_index, blocks, parity):
    clamped = jnp.clip(block_index, 0, blocks - 1)
    return jnp.where(parity == 0, clamped, blocks - 1 - clamped)


def local(design, cotangent):
    layers, tile_rows, tile_cols = design.shape
    build_count = lax.axis_size("build")
    build_index = lax.axis_index("build")
    parity = lax.axis_index("gx") % 2
    blocks = 4
    height = tile_rows // blocks
    span_rows = height + 2 * layers
    span_cols = tile_cols + 2 * layers
    row_global = lax.axis_index("gx") * tile_rows - layers + jnp.arange(tile_rows + 2 * layers)
    col_global = lax.axis_index("gy") * tile_cols - layers + jnp.arange(span_cols)
    row_inside = ((row_global >= 0) & (row_global < tile_rows * lax.axis_size("gx"))).astype(
        jnp.float32
    )
    col_inside = ((col_global >= 0) & (col_global < tile_cols * lax.axis_size("gy"))).astype(
        jnp.float32
    )
    inside_pad = row_inside[:, None] * col_inside[None, :]
    widened = widen_deep(jnp.concatenate([design, cotangent], 0), layers)
    design_pad = widened[:layers]
    cotangent_pad = widened[layers:]
    step_count = blocks + 2 * (build_count - 1)
    plate = jnp.where(build_index == 0, 1.0, 0.0).astype(jnp.float32)
    buffer_start = plate * jnp.ones((tile_rows, tile_cols), jnp.float32)
    printed_start = jnp.zeros((layers, tile_rows, tile_cols), jnp.float32)

    def forward_step(step_index, carried):
        buffer, printed = carried
        padded = extend(buffer, layers)
        block_index = step_index - 2 * build_index
        row_start = block_place(block_index, blocks, parity) * height

        def forward_compute(printed):
            support = lax.dynamic_slice(padded, (row_start, 0), (span_rows, span_cols))
            designs = lax.dynamic_slice(
                design_pad, (0, row_start, 0), (layers, span_rows, span_cols)
            )
            inside = lax.dynamic_slice(inside_pad, (row_start, 0), (span_rows, span_cols))
            pieces = []
            for stratum in range(layers):
                totals = shifted_sum(jnp.exp(SHARPNESS * support))
                bounds = jnp.log(totals / 5.0) / SHARPNESS
                excess = designs[stratum] - bounds
                radius = jnp.sqrt(excess * excess + SOFTNESS)
                support = 0.5 * (designs[stratum] + bounds - radius + SOFT_ROOT) * inside
                pieces.append(support[layers : layers + height, layers : layers + tile_cols])
            return lax.dynamic_update_slice(printed, jnp.stack(pieces), (0, row_start, 0))

        def forward_unchanged(printed):
            return printed

        active = (block_index >= 0) & (block_index < blocks)
        printed = lax.cond(active, forward_compute, forward_unchanged, printed)
        top_rows = lax.dynamic_slice(printed, (layers - 1, row_start, 0), (1, height, tile_cols))[0]
        received = shifted(top_rows, "build", 1)
        arrival = block_index + 2
        landing = block_place(arrival, blocks, parity) * height
        placed = lax.dynamic_update_slice(buffer, received, (landing, 0))
        usable = (build_index > 0) & (arrival >= 0) & (arrival < blocks)
        buffer = jnp.where(usable, placed, buffer)
        return (buffer, printed)

    buffer, printed = lax.fori_loop(0, step_count, forward_step, (buffer_start, printed_start))
    density_pad = widen_deep(jnp.concatenate([buffer[None], printed], 0), layers)
    above_start = jnp.zeros((tile_rows, tile_cols), jnp.float32)
    gradient_start = jnp.zeros((layers, tile_rows, tile_cols), jnp.float32)

    def adjoint_step(step_index, carried):
        above, gradient = carried
        padded = extend(above, layers)
        block_index = step_index - 2 * (build_count - 1 - build_index)
        row_start = block_place(block_index, blocks, parity) * height

        def adjoint_compute(gradient):
            upper = lax.dynamic_slice(padded, (row_start, 0), (span_rows, span_cols))
            densities = lax.dynamic_slice(
                density_pad, (0, row_start, 0), (layers + 1, span_rows, span_cols)
            )
            designs = lax.dynamic_slice(
                design_pad, (0, row_start, 0), (layers, span_rows, span_cols)
            )
            cotangents = lax.dynamic_slice(
                cotangent_pad, (0, row_start, 0), (layers, span_rows, span_cols)
            )
            inside = lax.dynamic_slice(inside_pad, (row_start, 0), (span_rows, span_cols))
            weights = jnp.exp(SHARPNESS * densities)
            pieces = []
            for stratum in range(layers - 1, -1, -1):
                totals = shifted_sum(weights[stratum])
                bounds = jnp.log(totals / 5.0) / SHARPNESS
                excess = designs[stratum] - bounds
                radius = jnp.sqrt(excess * excess + SOFTNESS)
                adjoint = cotangents[stratum] + weights[stratum + 1] * shifted_sum(upper)
                local_gradient = adjoint * 0.5 * (1.0 - excess / radius)
                pieces.append(local_gradient[layers : layers + height, layers : layers + tile_cols])
                upper = adjoint * 0.5 * (1.0 + excess / radius) / totals * inside
            ordered = jnp.stack(pieces[::-1])
            updated = lax.dynamic_update_slice(gradient, ordered, (0, row_start, 0))
            return (updated, upper[layers : layers + height, layers : layers + tile_cols])

        def adjoint_unchanged(gradient):
            return (gradient, jnp.zeros((height, tile_cols), jnp.float32))

        active = (block_index >= 0) & (block_index < blocks)
        gradient, lower_rows = lax.cond(active, adjoint_compute, adjoint_unchanged, gradient)
        received = shifted(lower_rows, "build", -1)
        arrival = block_index + 2
        landing = block_place(arrival, blocks, parity) * height
        placed = lax.dynamic_update_slice(above, received, (landing, 0))
        usable = (build_index < build_count - 1) & (arrival >= 0) & (arrival < blocks)
        above = jnp.where(usable, placed, above)
        return (above, gradient)

    above, gradient = lax.fori_loop(0, step_count, adjoint_step, (above_start, gradient_start))
    return (printed, gradient)


def solution(mesh):
    in_specs = (P("build", "gx", "gy"), P("build", "gx", "gy"))
    out_specs = (P("build", "gx", "gy"), P("build", "gx", "gy"))
    return jax.shard_map(local, mesh=mesh, in_specs=in_specs, out_specs=out_specs, check_vma=False)
```

profile of v0, /device:TPU:126, one launch (start us, length us, event | category | flops | bytes accessed | tf_op | source)
XLA Modules:
  0.0 1527.3 jit_solution(12893436386698964500)
XLA Ops:
  20.9 743.6 %while.42 = (s32[]{:T(128)}, f32[64,256]{1,0:T(8,128)S(1)}, f32[4,64,256]{2,1,0:T(8,128)S(1)}, s32[]{:T(128)}, pred[]{:T(512)}, /*index=5*/pred[]{:T(512)}, f32[...) while((s32[]{:T(128)}, f32[64,256]{1,0:T(8,128)S(1)}, ...), condition=%wide.region_3.4_spmd.clone, body=%wide.region_0.3_spmd.clone.sunk | while | flops 551908 | bytes 1463661 | solution.py:116
  36.3 5.0 collective-permute-start.4
  58.0 5.4 collective-permute-start.4
  79.8 5.4 collective-permute-start.4
  101.5 5.4 collective-permute-start.4
  123.2 5.4 collective-permute-start.4
  145.0 5.4 collective-permute-start.4
  211.2 5.4 collective-permute-start.4
  234.0 5.4 collective-permute-start.4
  255.7 6.5 collective-permute-start.4
  278.5 6.5 collective-permute-start.4
  301.3 5.4 collective-permute-start.4
  323.0 5.4 collective-permute-start.4
  344.7 5.4 collective-permute-start.4
  366.5 5.4 collective-permute-start.4
  388.2 5.4 collective-permute-start.4
  409.9 5.4 collective-permute-start.4
  431.7 5.4 collective-permute-start.4
  453.4 5.4 collective-permute-start.4
  475.1 5.4 collective-permute-start.4
  496.9 5.4 collective-permute-start.4
  518.6 5.4 collective-permute-start.4
  540.3 5.4 collective-permute-start.4
  562.1 5.4 collective-permute-start.4
  583.8 5.4 collective-permute-start.4
  605.5 5.4 collective-permute-start.4
  627.3 5.4 collective-permute-start.4
  649.0 5.4 collective-permute-start.4
  670.7 5.4 collective-permute-start.4
  692.5 5.4 collective-permute-start.4
  714.2 5.4 collective-permute-start.4
  735.9 5.4 collective-permute-start.4
  757.7 5.4 collective-permute-start.4
  781.4 745.2 %while.43 = (s32[]{:T(128)}, f32[64,256]{1,0:T(8,128)S(1)}, f32[4,64,256]{2,1,0:T(8,128)S(1)}, s32[]{:T(128)}, pred[]{:T(512)}, /*index=5*/pred[]{:T(512)}, f32[...) while((s32[]{:T(128)}, f32[64,256]{1,0:T(8,128)S(1)}, ...), condition=%wide.region_7.8_spmd.clone, body=%wide.region_4.7_spmd.clone.sunk | while | flops 772897 | bytes 2201723 | solution.py:167
  798.3 5.2 collective-permute-done.9
  820.3 4.9 collective-permute-done.9
  842.0 4.9 collective-permute-done.9
  863.7 4.9 collective-permute-done.9
  885.5 4.9 collective-permute-done.9
  907.2 4.9 collective-permute-done.9
  928.9 4.9 collective-permute-done.9
  950.7 4.9 collective-permute-done.9
  972.4 4.9 collective-permute-done.9
  994.1 4.9 collective-permute-done.9
  1015.9 4.9 collective-permute-done.9
  1037.6 4.9 collective-permute-done.9
  1059.3 4.9 collective-permute-done.9
  1081.0 4.9 collective-permute-done.9
  1102.8 4.9 collective-permute-done.9
  1124.5 4.9 collective-permute-done.9
  1146.2 4.9 collective-permute-done.9
  1168.0 4.9 collective-permute-done.9
  1189.7 4.9 collective-permute-done.9
  1211.4 4.9 collective-permute-done.9
  1233.2 4.9 collective-permute-done.9
  1254.9 5.5 collective-permute-done.9
  1277.2 6.7 collective-permute-done.9
  1300.7 4.9 collective-permute-done.9
  1346.0 4.9 collective-permute-done.9
  1368.7 4.9 collective-permute-done.9
  1391.3 4.9 collective-permute-done.9
  1413.1 4.9 collective-permute-done.9
  1434.8 4.9 collective-permute-done.9
  1456.5 4.9 collective-permute-done.9
  (1217 shorter events, 1201.3 us)
Async XLA Ops:
  12.3 8.0 collective-permute-start.12
  58.0 6.9 collective-permute-start.4
  79.8 6.9 collective-permute-start.4
  101.5 6.9 collective-permute-start.4
  123.2 6.9 collective-permute-start.4
  145.0 6.9 collective-permute-start.4
  234.0 6.9 collective-permute-start.4
  255.7 7.9 collective-permute-start.4
  278.5 7.9 collective-permute-start.4
  301.3 6.9 collective-permute-start.4
  323.0 6.9 collective-permute-start.4
  344.7 6.9 collective-permute-start.4
  366.5 6.9 collective-permute-start.4
  388.2 6.9 collective-permute-start.4
  409.9 6.9 collective-permute-start.4
  431.7 6.9 collective-permute-start.4
  453.4 6.9 collective-permute-start.4
  475.1 6.9 collective-permute-start.4
  496.9 6.9 collective-permute-start.4
  518.6 6.9 collective-permute-start.4
  540.3 6.9 collective-permute-start.4
  562.1 6.9 collective-permute-start.4
  583.8 6.9 collective-permute-start.4
  605.5 6.9 collective-permute-start.4
  627.3 6.9 collective-permute-start.4
  649.0 6.9 collective-permute-start.4
  670.7 6.9 collective-permute-start.4
  692.5 6.9 collective-permute-start.4
  714.2 6.9 collective-permute-start.4
  735.9 6.9 collective-permute-start.4
  757.7 6.9 collective-permute-start.4
  774.2 6.9 collective-permute-start.16
  796.3 7.1 collective-permute-start.9
  818.3 6.8 collective-permute-start.9
  840.1 6.8 collective-permute-start.9
  861.8 6.8 collective-permute-start.9
  883.5 6.8 collective-permute-start.9
  905.3 6.8 collective-permute-start.9
  927.0 6.8 collective-permute-start.9
  948.7 6.8 collective-permute-start.9
  970.4 6.8 collective-permute-start.9
  992.2 6.8 collective-permute-start.9
  1013.9 6.8 collective-permute-start.9
  1035.6 6.8 collective-permute-start.9
  1057.4 6.8 collective-permute-start.9
  1079.1 6.8 collective-permute-start.9
  1100.8 6.8 collective-permute-start.9
  1122.6 6.8 collective-permute-start.9
  1144.3 6.8 collective-permute-start.9
  1166.0 6.8 collective-permute-start.9
  1187.7 6.8 collective-permute-start.9
  1209.5 6.8 collective-permute-start.9
  1231.2 6.8 collective-permute-start.9
  1252.9 7.4 collective-permute-start.9
  1275.2 8.7 collective-permute-start.9
  1298.8 6.8 collective-permute-start.9
  1321.4 6.8 collective-permute-start.9
  1344.1 6.8 collective-permute-start.9
  1366.7 6.8 collective-permute-start.9
  1389.4 6.8 collective-permute-start.9
  1411.1 6.8 collective-permute-start.9
  1432.8 6.8 collective-permute-start.9
  1454.6 6.8 collective-permute-start.9
  1476.3 6.8 collective-permute-start.9
  (287 other events, 1337.0 us)
where the time goes:
time: 1540 us; the launch traced here: 1530 us
  starting transfers between devices  778 us (51%)
  waiting for transfers between devices  714 us (46%)
    ppermute x140, waiting for transfers between devices, extended(): before = lax.ppermute(last, axis, up)  494 us
    ppermute x140, starting transfers between devices, extended(): after = lax.ppermute(initial, axis, down)  270 us
    ppermute x140, starting transfers between devices, extended(): before = lax.ppermute(last, axis, up)  259 us
    ppermute x68, starting transfers between devices, shifted(): lax.ppermute(value, axis, [(source, source + steps) for source in range(i...  249 us
    ppermute x68, waiting for transfers between devices, shifted(): lax.ppermute(value, axis, [(source, source + steps) for source in range(i...  216 us
  transfers between devices with their start and end apart: 348, of which 212 were waited for; matrix products, arithmetic and copies ran while one was open for 0% of the time, Pallas kernels for 0%

commit v1 on v0

v1 whole, which is shorter than its diff:
```python
import math

import jax
import jax.numpy as jnp
from jax import lax
from jax.experimental import pallas as pl
from jax.experimental.pallas import tpu as pltpu
from jax.sharding import PartitionSpec as P

MESH = pl.DeviceIdType.MESH
SHARPNESS = 40.0
SOFTNESS = 0.0001
SOFT_ROOT = 0.01
LOG2_E = 1.0 / math.log(2.0)

GROUP = 4
OWN = 4
DEPTH = GROUP * OWN
ROWS = 64
COLS = 256
BAND = ROWS // GROUP
REGION = 3 * BAND
WIDE = COLS + 128
KEPT = 7
LATE = DEPTH - KEPT


def five(v):
    rows = v.shape[0]
    return (
        v
        + pltpu.roll(v, 1, axis=0)
        + pltpu.roll(v, rows - 1, axis=0)
        + pltpu.roll(v, 1, axis=1)
        + pltpu.roll(v, WIDE - 1, axis=1)
    )


def kernel(
    d_ref, c_ref, pr_ref, gr_ref,
    edge, edge_in, wrap, big, bigwrap, weights, ends, ends_in, late_ends, late_in,
    top, top_in, pst, gst, a1, a2, inside_ref,
    swap_s, swap_r, wrap_s, wrap_r, edge_s, edge_r, hand_s, hand_r, back_s, back_r,
    late_s, late_r, out_s, out_r,
):
    zb, y, g = lax.axis_index("build"), lax.axis_index("gx"), lax.axis_index("gy")
    stages, gys = lax.axis_size("build") // GROUP, lax.axis_size("gy")
    blocks = lax.axis_size("gx") * GROUP
    s, place = zb // GROUP, zb % GROUP

    def flip(row, v):
        return v + (row % 2) * (GROUP - 1 - 2 * v)

    r = flip(y, place)
    block = GROUP * y + r

    def owner(stage, blk, gy):
        row = blk // GROUP
        return {"build": GROUP * stage + flip(row, blk % GROUP), "gx": row, "gy": gy}

    def start(src, dst, send, recv, dev):
        pltpu.make_async_remote_copy(
            src_ref=src, dst_ref=dst, send_sem=send, recv_sem=recv, device_id=dev, device_id_type=MESH
        ).start()

    def wait(ref, sem):
        pltpu.make_async_copy(ref, ref, sem).wait()

    def flag(c):
        return jnp.where(c, 1, 0)

    barrier = pltpu.get_barrier_semaphore()
    count = jnp.int32(0)

    def greet(dev, valid):
        @pl.when(valid)
        def _():
            pl.semaphore_signal(barrier, inc=1, device_id=dev, device_id_type=MESH)

        return flag(valid)

    def near(blk, gy):
        return (blk >= 0) & (blk < blocks) & (gy >= 0) & (gy < gys)

    for dy in (-1, 0, 1):
        for p in range(GROUP):
            valid = (y + dy >= 0) & (y + dy < blocks // GROUP)
            if dy == 0:
                valid = valid & (p != place)
            count += greet({"build": GROUP * s + p, "gx": y + dy, "gy": g}, valid)
    for dg in (-1, 1):
        for db in (-1, 0, 1):
            count += greet(owner(s, block + db, g + dg), near(block + db, g + dg))
    for ds in (-1, 1):
        for dg in (-1, 0, 1):
            for db in (-1, 0, 1):
                valid = near(block + db, g + dg) & (s + ds >= 0) & (s + ds < stages)
                count += greet(owner(s + ds, block + db, g + dg), valid)

    lane = lax.broadcasted_iota(jnp.int32, (ROWS, 128), 1)
    for which, ref in enumerate((d_ref, c_ref)):
        packed = jnp.zeros((ROWS, 128), jnp.float32)
        for i in range(OWN):
            both = jnp.where(lane < 64, ref[i, :, 0:128], ref[i, :, 128:256])
            if i:
                both = pltpu.roll(both, 32 * i, axis=1)
            slot = (lane + 16 - 32 * i + 128) % 128
            packed = jnp.where(slot < 32, both, packed)
        edge[which] = packed
    row = lax.broadcasted_iota(jnp.int32, (REGION, WIDE), 0) + (block - 1) * BAND
    col = lax.broadcasted_iota(jnp.int32, (REGION, WIDE), 1)
    col = jnp.where(col < COLS + 64, col, col - WIDE) + g * COLS
    within = (row >= 0) & (row < blocks * BAND) & (col >= 0) & (col < gys * COLS)
    inside_ref[...] = jnp.where(within, 1.0, 0.0)

    pl.semaphore_wait(barrier, count)

    def edge_send(which, go):
        for side, dg in ((0, 1), (1, -1)):

            @pl.when((g + dg >= 0) & (g + dg < gys))
            def _():
                if go:
                    start(edge.at[which], edge_in.at[which, side], edge_s.at[which, side], edge_r.at[which, side],
                          {"build": zb, "gx": y, "gy": g + dg})
                else:
                    wait(edge.at[which], edge_s.at[which, side])

    def edge_land(which):
        for side, dg in ((0, -1), (1, 1)):

            @pl.when((g + dg >= 0) & (g + dg < gys))
            def _():
                wait(edge_in.at[which, side], edge_r.at[which, side])

        wrap[which] = jnp.where(lane % 32 < 16, edge_in[which, 1], edge_in[which, 0])

    def swap(which, narrow, go):
        def step(rp, _):
            rows = pl.ds(pl.multiple_of(rp * BAND, BAND), BAND)
            for db in (-1, 0, 1):
                target = GROUP * y + rp + db
                there = pl.ds((1 - db) * BAND, BAND)
                if narrow:
                    src = wrap.at[which, rows]
                    dst = bigwrap.at[which, place, there]
                    send, recv = wrap_s.at[which, rp, db + 1], wrap_r.at[which, place, 1 - db]
                else:
                    src = (d_ref, c_ref)[which].at[:, rows]
                    dst = big.at[which, pl.ds(OWN * place, OWN), there]
                    send, recv = swap_s.at[which, rp, db + 1], swap_r.at[which, place, 1 - db]

                @pl.when((target >= 0) & (target < blocks) & (target != block))
                def _():
                    if go:
                        start(src, dst, send, recv, owner(s, target, g))
                    else:
                        wait(src, send)

                if go:

                    @pl.when(target == block)
                    def _():
                        pltpu.make_async_copy(src, dst, recv).start()

            return 0

        lax.fori_loop(0, GROUP, step, 0)

    def swap_land(which, p):
        for b in range(3):
            there = pl.ds(b * BAND, BAND)

            @pl.when((block + b - 1 >= 0) & (block + b - 1 < blocks))
            def _():
                wait(big.at[which, pl.ds(OWN * p, OWN), there], swap_r.at[which, p, b])
                wait(bigwrap.at[which, p, there], wrap_r.at[which, p, b])

    edge_send(0, True)
    swap(0, False, True)
    edge_send(1, True)
    edge_land(0)
    swap(0, True, True)
    swap(1, False, True)
    edge_land(1)
    swap(1, True, True)

    def hand(up, go):
        which = 0 if up else 1
        ds = 1 if up else -1
        send = hand_s if up else back_s
        recv = hand_r if up else back_r
        for db in (-1, 0, 1):
            for dg in (0, -1, 1):
                there = pl.ds((1 - db) * BAND, BAND)
                if dg == 0:
                    src, dst = top.at[which], top_in.at[which, there]
                else:
                    src, dst = ends.at[which], ends_in.at[which, 0 if dg == 1 else 1, there]

                @pl.when(near(block + db, g + dg) & (s + ds >= 0) & (s + ds < stages))
                def _():
                    if go:
                        start(src, dst, send.at[1 - db, 1 - dg], recv.at[1 - db, 1 - dg],
                              owner(s + ds, block + db, g + dg))
                    else:
                        wait(src, send.at[1 - db, 1 - dg])

    def hand_land(up):
        which = 0 if up else 1
        ds = -1 if up else 1
        recv = hand_r if up else back_r
        for b in range(3):
            for e in range(3):
                there = pl.ds(b * BAND, BAND)
                if e == 1:
                    dst = top_in.at[which, there]
                else:
                    dst = ends_in.at[which, 0 if e == 0 else 1, there]

                @pl.when(near(block + b - 1, g + e - 1) & (s + ds >= 0) & (s + ds < stages))
                def _():
                    wait(dst, recv.at[b, e])

    lane_region = lax.broadcasted_iota(jnp.int32, (REGION, 128), 1)
    lane_band = lax.broadcasted_iota(jnp.int32, (BAND, 128), 1)

    def handed(which):
        tail = jnp.where(lane_region < 64, ends_in[which, 1], ends_in[which, 0])
        return jnp.concatenate([top_in[which], tail], axis=1)

    def give(which, value):
        top[which] = value
        ends[which] = jnp.where(lane_band < 64, value[:, 0:128], value[:, 128:256])

    def field(which, p, i, lo, hi):
        tail = bigwrap[which, p, lo:hi]
        if i:
            tail = pltpu.roll(tail, 128 - 32 * i, axis=1)
        return jnp.concatenate([big[which, OWN * p + i, lo:hi], tail], axis=1)

    def terms(total, des):
        bound = jnp.log2(total) * (1.0 / (LOG2_E * SHARPNESS)) - math.log(5.0) / SHARPNESS
        excess = des - bound
        under = excess * excess + SOFTNESS
        return bound, excess, under, lax.rsqrt(under)

    hand_land(True)
    inside = inside_ref[...] > 0.5
    first = jnp.where(s > 0, handed(0), jnp.full((REGION, WIDE), math.exp(SHARPNESS), jnp.float32))
    first = jnp.where(inside, first, 1.0)
    weights[0] = first

    def forward(lo, hi, p, w):
        swap_land(0, p)
        mask = inside_ref[lo:hi] > 0.5
        for i in range(OWN):
            des = field(0, p, i, lo, hi)
            bound, excess, under, inverse = terms(five(w), des)
            fresh = 0.5 * (des + bound - under * inverse + SOFT_ROOT)
            w = jnp.where(mask, jnp.exp2(fresh * (SHARPNESS * LOG2_E)), 1.0)
            pst[OWN * p + i] = fresh[BAND - lo : 2 * BAND - lo, 0:COLS]
            j = OWN * p + i
            if lo == 0 and i < OWN - 1:
                weights[j + 1] = w
            elif lo == 0:

                @pl.when(p == 0)
                def _():
                    weights[j + 1] = w

                @pl.when(p > 0)
                def _():
                    weights[j + 1, BAND : 2 * BAND, 0:COLS] = w[BAND : 2 * BAND, 0:COLS]

            else:
                weights[j + 1, BAND : 2 * BAND, 0:COLS] = w[BAND - lo : 2 * BAND - lo, 0:COLS]
        return w

    half = BAND // 2
    w = lax.fori_loop(0, 2, lambda p, w: forward(0, REGION, p, w), first)
    w = w[half : REGION - half]
    w = lax.fori_loop(2, 4, lambda p, w: forward(half, REGION - half, p, w), w)
    give(0, w[half : half + BAND, 0:COLS])
    hand(True, True)

    own = weights[KEPT + 1 :, BAND : 2 * BAND, 0:COLS]
    lane_late = lax.broadcasted_iota(jnp.int32, (LATE, BAND, 128), 2)
    late_ends[...] = jnp.where(lane_late < 64, own[:, :, 0:128], own[:, :, 128:256])

    def late(go):
        for db in (-1, 0, 1):
            for dg in (0, -1, 1):
                if db == 0 and dg == 0:
                    continue
                there = pl.ds((1 - db) * BAND, BAND)
                if dg == 0:
                    src = weights.at[pl.ds(KEPT + 1, LATE), pl.ds(BAND, BAND), pl.ds(0, COLS)]
                    dst = weights.at[pl.ds(KEPT + 1, LATE), there, pl.ds(0, COLS)]
                else:
                    src, dst = late_ends, late_in.at[0 if dg == 1 else 1, :, there]

                @pl.when(near(block + db, g + dg))
                def _():
                    if go:
                        start(src, dst, late_s.at[1 - db, 1 - dg], late_r.at[1 - db, 1 - dg],
                              owner(s, block + db, g + dg))
                    else:
                        wait(src, late_s.at[1 - db, 1 - dg])

    def late_land():
        for b in range(3):
            for e in range(3):
                if b == 1 and e == 1:
                    continue
                there = pl.ds(b * BAND, BAND)
                if e == 1:
                    dst = weights.at[pl.ds(KEPT + 1, LATE), there, pl.ds(0, COLS)]
                else:
                    dst = late_in.at[0 if e == 0 else 1, :, there]

                @pl.when(near(block + b - 1, g + e - 1))
                def _():
                    wait(dst, late_r.at[b, e])

    late(True)

    def result(which, p, go):
        src_ref, dst_ref = (pst, gst)[which], (pr_ref, gr_ref)[which]
        src = src_ref.at[pl.ds(OWN * p, OWN)]
        dst = dst_ref.at[:, pl.ds(pl.multiple_of(r * BAND, BAND), BAND)]

        @pl.when(p != place)
        def _():
            if go:
                start(src, dst, out_s.at[which, p], out_r.at[which, r], {"build": GROUP * s + p, "gx": y, "gy": g})
            else:
                wait(src, out_s.at[which, p])

        if go:

            @pl.when(p == place)
            def _():
                pltpu.make_async_copy(src, dst, out_r.at[which, r]).start()

    for p in range(GROUP):
        result(0, p, True)

    late_land()

    def fill(n, _):
        j = n + KEPT + 1
        tail = jnp.where(lane_region < 64, late_in[1, n], late_in[0, n])
        weights[j, :, COLS:] = jnp.where(inside_ref[:, COLS:] > 0.5, tail, 1.0)
        for rows in (slice(0, BAND), slice(2 * BAND, REGION)):
            weights[j, rows, 0:COLS] = jnp.where(inside_ref[rows, 0:COLS] > 0.5, weights[j, rows, 0:COLS], 1.0)
        return 0

    lax.fori_loop(0, LATE, fill, 0)

    def prepare(lo, hi, p, _):
        for i in range(OWN):
            j = OWN * p + i
            total = five(weights[j, lo:hi])
            bound, excess, under, inverse = terms(total, field(0, p, i, lo, hi))
            ratio = excess * inverse
            a1[j, lo:hi] = jnp.where(inside_ref[lo:hi] > 0.5, 0.5 * (1.0 + ratio) / total, 0.0)
            a2[j] = 0.5 * (1.0 - ratio[BAND - lo : 2 * BAND - lo, 0:COLS])
        return 0

    lax.fori_loop(0, 2, lambda p, _: prepare(half, REGION - half, p, _), 0)
    lax.fori_loop(2, 4, lambda p, _: prepare(0, REGION, p, _), 0)

    for p in range(GROUP):
        swap_land(1, p)
    hand_land(False)
    q = jnp.where((s < stages - 1) & inside, handed(1), 0.0)

    def backward(lo, hi, n, q):
        p = GROUP - 1 - n
        mask = inside_ref[lo:hi] > 0.5
        for i in range(OWN - 1, -1, -1):
            j = OWN * p + i
            adjoint = field(1, p, i, lo, hi) + weights[j + 1, lo:hi] * five(q)
            gst[j] = adjoint[BAND - lo : 2 * BAND - lo, 0:COLS] * a2[j]
            q = jnp.where(mask, adjoint * a1[j, lo:hi], 0.0)
        return q

    q = lax.fori_loop(0, 2, lambda n, q: backward(0, REGION, n, q), q)
    q = q[half : REGION - half]
    q = lax.fori_loop(2, 4, lambda n, q: backward(half, REGION - half, n, q), q)
    give(1, q[half : half + BAND, 0:COLS])
    hand(False, True)
    for p in range(GROUP):
        result(1, p, True)

    for which in range(2):
        edge_send(which, False)
        swap(which, False, False)
        swap(which, True, False)
        for p in range(GROUP):
            result(which, p, False)
    hand(True, False)
    hand(False, False)
    late(False)
    for which in range(2):
        for p in range(GROUP):
            rows = pl.ds(BAND * p, BAND)
            wait((pr_ref, gr_ref)[which].at[:, rows], out_r.at[which, p])


def local(design, cotangent):
    shard = jax.ShapeDtypeStruct(design.shape, jnp.float32)
    f32 = lambda *shape: pltpu.VMEM(shape, jnp.float32)
    dma = lambda *shape: pltpu.SemaphoreType.DMA(shape)
    vmem = pl.BlockSpec(memory_space=pltpu.VMEM)
    return pl.pallas_call(
        kernel,
        out_shape=(shard, shard),
        in_specs=[vmem, vmem],
        out_specs=(vmem, vmem),
        scratch_shapes=[
            f32(2, ROWS, 128),
            f32(2, 2, ROWS, 128),
            f32(2, ROWS, 128),
            f32(2, DEPTH, REGION, COLS),
            f32(2, GROUP, REGION, 128),
            f32(DEPTH + 1, REGION, WIDE),
            f32(2, BAND, 128),
            f32(2, 2, REGION, 128),
            f32(LATE, BAND, 128),
            f32(2, LATE, REGION, 128),
            f32(2, BAND, COLS),
            f32(2, REGION, COLS),
            f32(DEPTH, BAND, COLS),
            f32(DEPTH, BAND, COLS),
            f32(DEPTH, REGION, WIDE),
            f32(DEPTH, BAND, COLS),
            f32(REGION, WIDE),
            dma(2, GROUP, 3),
            dma(2, GROUP, 3),
            dma(2, GROUP, 3),
            dma(2, GROUP, 3),
            dma(2, 2),
            dma(2, 2),
            dma(3, 3),
            dma(3, 3),
            dma(3, 3),
            dma(3, 3),
            dma(3, 3),
            dma(3, 3),
            dma(2, GROUP),
            dma(2, GROUP),
        ],
        compiler_params=pltpu.CompilerParams(
            collective_id=0, has_side_effects=True, vmem_limit_bytes=40 * 1024 * 1024
        ),
    )(design, cotangent)


def solution(mesh):
    spec = P("build", "gx", "gy")
    return jax.shard_map(local, mesh=mesh, in_specs=(spec, spec), out_specs=(spec, spec), check_vma=False)
```

time: 1540 us -> 147 us (0.10)
  the two profiles are of different devices: /device:TPU:126 before, /device:TPU:18 now
where the time goes in v1:
time: 147 us; the launch traced here: 146 us
  Pallas kernels  142 us (97%)
  local copies, waits for them, and re-layouts  3.3 us (2%)
    pallas_call x1, Pallas kernels, local(): pl.pallas_call(kernel, out_shape=(shard, shard), in_specs=[vmem, vmem], o...  142 us
    unnamed x6, local copies, waits for them, and re-layouts  3.3 us

profile of v1, /device:TPU:18, one launch (start us, length us, event | category | flops | bytes accessed | tf_op | source)
XLA Modules:
  0.0 146.4 jit_solution(6885734655321895231)
XLA Ops:
  0.6 0.0 copy-start
  0.6 0.9 copy-done
  1.6 0.0 copy-start.1
  1.6 0.9 copy-done.1
  2.5 142.5 %shard_map.41 = (f32[4,64,256]{2,1,0:T(8,128)S(1)}, f32[4,64,256]{2,1,0:T(8,128)S(1)}) custom-call(f32[4,64,256]{2,1,0:T(8,128)S(1)} %copy-done, f32[4,64,256]{2,1,0:T(8,128)S(1)} %copy-done.1), custom_call_target="tpu_custom_call" | custom-call | tf_op jit(solution)/shard_map/pallas_call | solution.py:417
  145.0 0.7 copy.6
  145.7 0.7 copy.7
Async XLA Ops:
  0.6 1.0 copy-start
  1.6 0.9 copy-start.1

commit v2 on v0

v2 whole, which is shorter than its diff:
```python
import math

import jax
import jax.numpy as jnp
from jax import lax
from jax.experimental import pallas as pl
from jax.experimental.pallas import tpu as pltpu
from jax.sharding import PartitionSpec as P

MESH = pl.DeviceIdType.MESH
SHARPNESS = 40.0
SOFTNESS = 0.0001
SOFT_ROOT = 0.01
LOG2_E = 1.0 / math.log(2.0)

OWN = 4
ROWS = 64
STRIP = 16
REGION = 3 * STRIP
LANES = 128
DEPTH = 16
PAIRS = DEPTH // 2
DESIGN, COTANGENT, WEIGHT = range(3)


def five(v):
    cols = v.shape[0]
    return (
        v
        + pltpu.roll(v, 1, axis=0)
        + pltpu.roll(v, cols - 1, axis=0)
        + pltpu.roll(v, 1, axis=1)
        + pltpu.roll(v, LANES - 1, axis=1)
    )


def turned(v, shift):
    return pltpu.roll(v, shift % LANES, axis=1) if shift % LANES else v


def kernel(
    d_ref, c_ref, pr_ref, gr_ref,
    raw, nat, ext, band_out, band_in, weights, a1, a2, results, home, sync_out, sync_in, inside_ref,
    raw_sem, swap_s, swap_r, col_s, col_r, band_s, band_r, sync_s, sync_r, out_s, out_r,
):
    z, y, g = lax.axis_index("build"), lax.axis_index("gx"), lax.axis_index("gy")
    planes, xs, gys = lax.axis_size("build"), lax.axis_size("gx"), lax.axis_size("gy")
    strips = planes * gys
    segments = planes * OWN // DEPTH
    per_segment = DEPTH // OWN

    def flip(column, v):
        return v + (column % 2) * (planes - 1 - 2 * v)

    k = flip(g, z)
    strip = planes * g + k

    def owner(number, row):
        column = number // planes
        return {"build": flip(column, number % planes), "gx": row, "gy": column}

    def near(ds, dy):
        return (strip + ds >= 0) & (strip + ds < strips) & (y + dy >= 0) & (y + dy < xs)

    def start(src, dst, send, recv, dev):
        pltpu.make_async_remote_copy(
            src_ref=src, dst_ref=dst, send_sem=send, recv_sem=recv, device_id=dev, device_id_type=MESH
        ).start()

    def wait(ref, sem):
        pltpu.make_async_copy(ref, ref, sem).wait()

    for which, ref in ((DESIGN, d_ref), (COTANGENT, c_ref)):
        pltpu.make_async_copy(ref, raw.at[which], raw_sem.at[which]).start()

    barrier = pltpu.get_barrier_semaphore()
    count = jnp.int32(planes - 1)

    def greet(p, _):
        @pl.when(p != z)
        def _():
            pl.semaphore_signal(barrier, inc=1, device_id={"build": p, "gx": y, "gy": g}, device_id_type=MESH)

        return 0

    lax.fori_loop(0, planes, greet, 0)
    for ds in (-1, 0, 1):
        for dy in (-1, 0, 1):
            if ds == 0 and dy == 0:
                continue
            valid = near(ds, dy)
            if dy == 0:
                valid = valid & ((strip + ds) // planes != g)

            @pl.when(valid)
            def _():
                pl.semaphore_signal(barrier, inc=1, device_id=owner(strip + ds, y + dy), device_id_type=MESH)

            count += jnp.where(valid, 1, 0)

    lane = lax.broadcasted_iota(jnp.int32, (REGION, LANES), 1)
    row = jnp.where(lane < 96, lane, lane - LANES) + y * ROWS
    col = lax.broadcasted_iota(jnp.int32, (REGION, LANES), 0) + (strip - 1) * STRIP
    within = (row >= 0) & (row < xs * ROWS) & (col >= 0) & (col < strips * STRIP)
    inside_ref[...] = jnp.where(within, 1.0, 0.0)

    def transpose_in(which):
        wait(raw.at[which], raw_sem.at[which])
        for n in range(OWN // 2):
            both = jnp.concatenate([raw[which, 2 * n], raw[which, 2 * n + 1]], axis=0)
            nat[which, n] = both.T

    transpose_in(DESIGN)
    pl.semaphore_wait(barrier, count)

    def swap(which, go):
        def step(i, _):
            p = (z + i) % planes
            src = nat.at[which, :, pl.ds(pl.multiple_of(flip(g, p) * STRIP, STRIP), STRIP)]
            dst = ext.at[which, pl.ds(2 * z, 2), pl.ds(STRIP, STRIP)]

            @pl.when(p != z)
            def _():
                if go:
                    start(src, dst, swap_s.at[which, p], swap_r.at[which, z], {"build": p, "gx": y, "gy": g})
                else:
                    wait(src, swap_s.at[which, p])

            if go:

                @pl.when(p == z)
                def _():
                    pltpu.make_async_copy(src, dst, swap_r.at[which, z]).start()

            return 0

        lax.fori_loop(0, planes, step, 0)

    def swap_land(which, seg):
        for i in range(per_segment):
            p = per_segment * seg + i
            wait(ext.at[which, pl.ds(2 * p, 2), pl.ds(STRIP, STRIP)], swap_r.at[which, p])

    def result(which, seg, go):
        def step(i, _):
            p = per_segment * seg + i
            src = results.at[which, pl.ds(2 * p, 2)]
            dst = home.at[which, :, pl.ds(pl.multiple_of(k * STRIP, STRIP), STRIP)]

            @pl.when(p != z)
            def _():
                if go:
                    start(src, dst, out_s.at[which, p], out_r.at[which, k], {"build": p, "gx": y, "gy": g})
                else:
                    wait(src, out_s.at[which, p])

            if go:

                @pl.when(p == z)
                def _():
                    pltpu.make_async_copy(src, dst, out_r.at[which, k]).start()

            return 0

        lax.fori_loop(0, per_segment, step, 0)

    def result_land(which):
        def step(n, _):
            there = pl.ds(pl.multiple_of(n * STRIP, STRIP), STRIP)
            wait(home.at[which, :, there], out_r.at[which, n])
            return 0

        lax.fori_loop(0, planes, step, 0)
        out = (pr_ref, gr_ref)[which]
        for n in range(OWN // 2):
            both = home[which, n].T
            out[2 * n] = both[0:ROWS]
            out[2 * n + 1] = both[ROWS:]

    def parts(which):
        if which == COTANGENT:
            return ((0, PAIRS // 2, STRIP // 2), (PAIRS // 2, PAIRS // 2, STRIP))
        if which == WEIGHT:
            return ((3, PAIRS - 3, STRIP),)
        return ((0, PAIRS, STRIP),)

    def columns(which, seg, go):
        for n, (first, number, width) in enumerate(parts(which)):
            pairs = pl.ds(PAIRS * seg + first, number)
            for side, ds in ((0, 1), (1, -1)):
                if side == 0:
                    here, there = pl.ds(2 * STRIP - width, width), pl.ds(STRIP - width, width)
                else:
                    here, there = pl.ds(STRIP, width), pl.ds(2 * STRIP, width)
                src, dst = ext.at[which, pairs, here], ext.at[which, pairs, there]

                @pl.when(near(ds, 0))
                def _():
                    if go:
                        start(src, dst, col_s.at[which, seg, n, side], col_r.at[which, seg, n, side],
                              owner(strip + ds, y))
                    else:
                        wait(src, col_s.at[which, seg, n, side])

    def columns_land(which, seg):
        for n, (first, number, width) in enumerate(parts(which)):
            pairs = pl.ds(PAIRS * seg + first, number)
            for side, ds in ((0, -1), (1, 1)):
                there = pl.ds(STRIP - width, width) if side == 0 else pl.ds(2 * STRIP, width)

                @pl.when(near(ds, 0))
                def _():
                    wait(ext.at[which, pairs, there], col_r.at[which, seg, n, side])

    def bands(which, seg, go):
        if go:
            for quad in range(2):
                for side in range(2):
                    packed = None
                    for m in range(4):
                        value = turned(ext[which, PAIRS * seg + 4 * quad + m], 16 * m)
                        if packed is None:
                            packed = value
                        else:
                            slot = (lane + (16 if side == 0 else 64) - 16 * m) % 64
                            packed = jnp.where(slot < 16, value, packed)
                    band_out[which, side, 2 * seg + quad] = packed
        for side, dy in ((0, 1), (1, -1)):
            src = band_out.at[which, side, pl.ds(2 * seg, 2)]
            dst = band_in.at[which, side, pl.ds(2 * seg, 2)]

            @pl.when(near(0, dy))
            def _():
                if go:
                    start(src, dst, band_s.at[which, seg, side], band_r.at[which, seg, side], owner(strip, y + dy))
                else:
                    wait(src, band_s.at[which, seg, side])

    def bands_land(which, seg):
        for side, dy in ((0, -1), (1, 1)):

            @pl.when(near(0, dy))
            def _():
                wait(band_in.at[which, side, pl.ds(2 * seg, 2)], band_r.at[which, seg, side])

    def field(which, pair, m, odd, lo, hi):
        lanes = lane[lo:hi]
        quad = pair // 4
        own = ext[which, pair, lo:hi]
        shift = -16 * m + (0 if odd else 64)
        above = turned(band_in[which, 0, quad, lo:hi], shift)
        below = turned(band_in[which, 1, quad, lo:hi], shift)
        return jnp.where(lanes < 64, turned(own, 64) if odd else own, jnp.where(lanes < 96, below, above))

    lane_own = lane[0:STRIP]

    def paired(even, odd):
        return jnp.where(lane_own < 64, even, turned(odd, 64))

    def sync(n, go):
        for ds in (-1, 0, 1):
            for dy in (-1, 0, 1):
                if ds == 0 and dy == 0:
                    continue
                src, dst = sync_out.at[n], sync_in.at[n, 1 - dy, pl.ds((1 - ds) * STRIP, STRIP)]

                @pl.when(near(ds, dy))
                def _():
                    if go:
                        start(src, dst, sync_s.at[n, 1 - dy, 1 - ds], sync_r.at[n, 1 - dy, 1 - ds],
                              owner(strip + ds, y + dy))
                    else:
                        wait(src, sync_s.at[n, 1 - dy, 1 - ds])

    def give(n, value):
        sync_out[n] = value
        sync(n, True)
        sync_in[n, 1, STRIP : 2 * STRIP] = value

    def taken(n, outside):
        for bs in range(3):
            for by in range(3):
                if bs == 1 and by == 1:
                    continue

                @pl.when(near(bs - 1, by - 1))
                def _():
                    wait(sync_in.at[n, by, pl.ds(bs * STRIP, STRIP)], sync_r.at[n, by, bs])

        above, below = turned(sync_in[n, 0], 64), turned(sync_in[n, 2], 64)
        whole = jnp.where(lane < 64, sync_in[n, 1], jnp.where(lane < 96, below, above))
        return jnp.where(inside_ref[...] > 0.5, whole, outside)

    def terms(total, des):
        bound = jnp.log2(total) * (1.0 / (LOG2_E * SHARPNESS)) - math.log(5.0) / SHARPNESS
        excess = des - bound
        under = excess * excess + SOFTNESS
        return bound, excess, under, lax.rsqrt(under)

    half = STRIP // 2
    narrow, wide = (half, REGION - half), (0, REGION)

    def own_of(v, lo):
        return v[STRIP - lo : 2 * STRIP - lo]

    def forward(seg, lo, hi, quad, w):
        mask = inside_ref[lo:hi] > 0.5
        for i in range(2):
            saved = []
            for odd in range(2):
                m = i
                pair = PAIRS * seg + 2 * quad + i
                layer = 2 * pair + odd
                des = field_dynamic(DESIGN, pair, quad, m, odd, lo, hi)
                bound, excess, under, inverse = terms(five(w), des)
                fresh = 0.5 * (des + bound - under * inverse + SOFT_ROOT)
                w = jnp.where(mask, jnp.exp2(fresh * (SHARPNESS * LOG2_E)), 1.0)
                weights[layer + 1, lo:hi] = w
                saved.append((own_of(w, lo), own_of(fresh, lo)))
            ext[WEIGHT, pair, STRIP : 2 * STRIP] = paired(saved[0][0], saved[1][0])
            results[0, pair] = paired(saved[0][1], saved[1][1])
        return w

    def field_dynamic(which, pair, part, i, odd, lo, hi):
        return field(which, pair, 2 * (part % 2) + i, odd, lo, hi)

    def forward_segment(seg, w):
        for part in range(4):
            lo, hi = wide if part < 2 else narrow
            if part == 2:
                w = w[half : REGION - half]
            w = forward(seg, lo, hi, part, w)
        return own_of(w, half)

    def fill(seg):
        bands_land(WEIGHT, seg)
        for n in range(3, PAIRS):
            for odd in range(2):
                value = field(WEIGHT, PAIRS * seg + n, n % 4, odd, 0, REGION)
                weights[DEPTH * seg + 2 * n + odd + 1] = jnp.where(inside_ref[...] > 0.5, value, 1.0)

    def prepare(seg):
        for j in range(DEPTH):
            lo, hi = narrow if j < DEPTH // 2 else wide
            layer, pair = DEPTH * seg + j, PAIRS * seg + j // 2
            total = five(weights[layer, lo:hi])
            bound, excess, under, inverse = terms(total, field(DESIGN, pair, (j // 2) % 4, j % 2, lo, hi))
            ratio = excess * inverse
            a1[layer, lo:hi] = jnp.where(inside_ref[lo:hi] > 0.5, 0.5 * (1.0 + ratio) / total, 0.0)
            a2[layer] = own_of(0.5 * (1.0 - ratio), lo)

    def backward_segment(seg, q):
        saved = None
        for j in range(DEPTH - 1, -1, -1):
            lo, hi = narrow if j < DEPTH // 2 else wide
            if j == DEPTH // 2 - 1:
                q = q[half : REGION - half]
            layer, pair = DEPTH * seg + j, PAIRS * seg + j // 2
            adjoint = field(COTANGENT, pair, (j // 2) % 4, j % 2, lo, hi) + weights[layer + 1, lo:hi] * five(q)
            q = jnp.where(inside_ref[lo:hi] > 0.5, adjoint * a1[layer, lo:hi], 0.0)
            slope = own_of(adjoint, lo) * a2[layer]
            if j % 2:
                saved = slope
            else:
                results[1, pair] = paired(slope, saved)
        return own_of(q, half)

    last = segments - 1
    swap(DESIGN, True)
    transpose_in(COTANGENT)
    swap_land(DESIGN, 0)
    columns(DESIGN, 0, True)
    columns_land(DESIGN, 0)
    bands(DESIGN, 0, True)
    swap(COTANGENT, True)
    if last > 0:
        swap_land(DESIGN, 1)
        columns(DESIGN, 1, True)
    for seg in range(segments):
        if seg == 0:
            w = jnp.where(inside_ref[...] > 0.5, math.exp(SHARPNESS), 1.0)
        else:
            w = taken(seg - 1, 1.0)
        weights[DEPTH * seg] = w
        bands_land(DESIGN, seg)
        w = forward_segment(seg, w)
        if seg < last:
            give(seg, w)
        columns(WEIGHT, seg, True)
        result(0, seg, True)
        if seg < last:
            columns_land(DESIGN, seg + 1)
            bands(DESIGN, seg + 1, True)
        if seg + 1 < last:
            swap_land(DESIGN, seg + 2)
            columns(DESIGN, seg + 2, True)
        if seg > 0:
            columns_land(WEIGHT, seg - 1)
            bands(WEIGHT, seg - 1, True)
        if seg == last - 1:
            swap_land(COTANGENT, last)
            columns(COTANGENT, last, True)

    if last == 0:
        swap_land(COTANGENT, last)
        columns(COTANGENT, last, True)
    columns_land(WEIGHT, last)
    bands(WEIGHT, last, True)
    columns_land(COTANGENT, last)
    bands(COTANGENT, last, True)
    if last > 0:
        swap_land(COTANGENT, last - 1)
        columns(COTANGENT, last - 1, True)
    fill(last)
    prepare(last)
    for seg in range(last, -1, -1):
        if seg == last:
            q = jnp.zeros((REGION, LANES), jnp.float32)
        else:
            q = taken(last + last - 1 - seg, 0.0)
        bands_land(COTANGENT, seg)
        q = backward_segment(seg, q)
        if seg > 0:
            give(last + last - seg, q)
        result(1, seg, True)
        if seg > 0:
            columns_land(COTANGENT, seg - 1)
            bands(COTANGENT, seg - 1, True)
            fill(seg - 1)
            prepare(seg - 1)
        if seg > 1:
            swap_land(COTANGENT, seg - 2)
            columns(COTANGENT, seg - 2, True)
        if seg == min(1, last):
            result_land(0)

    for which in (DESIGN, COTANGENT):
        swap(which, False)
    for seg in range(segments):
        for which in (DESIGN, COTANGENT, WEIGHT):
            columns(which, seg, False)
            bands(which, seg, False)
        for which in range(2):
            result(which, seg, False)
    for n in range(2 * last):
        sync(n, False)
    result_land(1)


def local(design, cotangent):
    shard = jax.ShapeDtypeStruct(design.shape, jnp.float32)
    planes = lax.axis_size("build")
    layers = planes * OWN
    segments = layers // DEPTH
    syncs = max(1, 2 * (segments - 1))
    f32 = lambda *shape: pltpu.VMEM(shape, jnp.float32)
    dma = lambda *shape: pltpu.SemaphoreType.DMA(shape)
    anywhere = pl.BlockSpec(memory_space=pl.ANY)
    vmem = pl.BlockSpec(memory_space=pltpu.VMEM)
    return pl.pallas_call(
        kernel,
        out_shape=(shard, shard),
        in_specs=[anywhere, anywhere],
        out_specs=(vmem, vmem),
        scratch_shapes=[
            f32(2, OWN, ROWS, planes * STRIP),
            f32(2, OWN // 2, planes * STRIP, LANES),
            f32(3, layers // 2, REGION, LANES),
            f32(3, 2, layers // 8, REGION, LANES),
            f32(3, 2, layers // 8, REGION, LANES),
            f32(layers + 1, REGION, LANES),
            f32(layers, REGION, LANES),
            f32(layers, STRIP, LANES),
            f32(2, layers // 2, STRIP, LANES),
            f32(2, OWN // 2, planes * STRIP, LANES),
            f32(syncs, STRIP, LANES),
            f32(syncs, 3, REGION, LANES),
            f32(REGION, LANES),
            dma(2),
            dma(2, planes),
            dma(2, planes),
            dma(3, segments, 2, 2),
            dma(3, segments, 2, 2),
            dma(3, segments, 2),
            dma(3, segments, 2),
            dma(syncs, 3, 3),
            dma(syncs, 3, 3),
            dma(2, planes),
            dma(2, planes),
        ],
        compiler_params=pltpu.CompilerParams(
            collective_id=0, has_side_effects=True, vmem_limit_bytes=40 * 1024 * 1024
        ),
    )(design, cotangent)


def solution(mesh):
    spec = P("build", "gx", "gy")
    return jax.shard_map(local, mesh=mesh, in_specs=(spec, spec), out_specs=(spec, spec), check_vma=False)
```

time: 1540 us -> 114 us (0.07)
  the two profiles are of different devices: /device:TPU:126 before, /device:TPU:8 now
where the time goes in v2:
time: 114 us
  Pallas kernels  110 us (96%)
  local copies, waits for them, and re-layouts  3.3 us (3%)
    pallas_call x1, Pallas kernels, local(): pl.pallas_call(kernel, out_shape=(shard, shard), in_specs=[anywhere, anyw...  110 us
    unnamed x6, local copies, waits for them, and re-layouts  3.3 us

profile of v2, /device:TPU:8, one launch (start us, length us, event | category | flops | bytes accessed | tf_op | source)
XLA Modules:
  0.0 114.2 jit_solution(3537482217732429755)
XLA Ops:
  0.6 0.0 copy-start
  0.6 0.9 copy-done
  1.6 0.0 copy-start.1
  1.6 0.9 copy-done.1
  2.5 110.3 %shard_map.41 = (f32[4,64,256]{2,1,0:T(8,128)S(1)}, f32[4,64,256]{2,1,0:T(8,128)S(1)}) custom-call(f32[4,64,256]{2,1,0:T(8,128)S(1)} %copy-done, f32[4,64,256]{2,1,0:T(8,128)S(1)} %copy-done.1), custom_call_target="tpu_custom_call" | custom-call | tf_op jit(solution)/shard_map/pallas_call | solution.py:460
  112.8 0.7 copy.6
  113.5 0.7 copy.7
Async XLA Ops:
  0.6 1.0 copy-start
  1.6 0.9 copy-start.1

commit v3 on v2

--- a/solution.py
+++ b/solution.py
@@ -12,9 +12,12 @@
 SOFTNESS = 0.0001
 SOFT_ROOT = 0.01
 LOG2_E = 1.0 / math.log(2.0)
+HALF = 0.5 * SHARPNESS * LOG2_E
 
 OWN = 4
 ROWS = 64
+EDGE = 8
+CHUNK = 64
 STRIP = 16
 REGION = 3 * STRIP
 LANES = 128
@@ -25,13 +28,9 @@
 
 def five(v):
     cols = v.shape[0]
-    return (
-        v
-        + pltpu.roll(v, 1, axis=0)
-        + pltpu.roll(v, cols - 1, axis=0)
-        + pltpu.roll(v, 1, axis=1)
-        + pltpu.roll(v, LANES - 1, axis=1)
-    )
+    by_row = pltpu.roll(v, 1, axis=1) + pltpu.roll(v, LANES - 1, axis=1)
+    by_col = pltpu.roll(v, 1, axis=0) + pltpu.roll(v, cols - 1, axis=0)
+    return by_row + (by_col + v)
 
 
 def turned(v, shift):
@@ -40,14 +39,18 @@
 
 def kernel(
     d_ref, c_ref, pr_ref, gr_ref,
-    raw, nat, ext, band_out, band_in, weights, a1, a2, results, home, sync_out, sync_in, inside_ref,
-    raw_sem, swap_s, swap_r, col_s, col_r, band_s, band_r, sync_s, sync_r, out_s, out_r,
+    raw, nat, ext, band_out, band_in, weights, a1, sync_out, sync_in, inside_ref,
+    nat_out, nat_in, border, pullbacks, nw, na1, na2, home,
+    raw_sem, swap_s, swap_r, col_s, col_r, band_s, band_r, sync_s, sync_r,
+    side_s, side_r, row_s, row_r, border_s, border_r, rim_s, rim_r,
 ):
     z, y, g = lax.axis_index("build"), lax.axis_index("gx"), lax.axis_index("gy")
     planes, xs, gys = lax.axis_size("build"), lax.axis_size("gx"), lax.axis_size("gy")
     strips = planes * gys
+    width = planes * STRIP
     segments = planes * OWN // DEPTH
     per_segment = DEPTH // OWN
+    last = segments - 1
 
     def flip(column, v):
         return v + (column % 2) * (planes - 1 - 2 * v)
@@ -88,15 +91,25 @@
         for dy in (-1, 0, 1):
             if ds == 0 and dy == 0:
                 continue
-            valid = near(ds, dy)
             if dy == 0:
-                valid = valid & ((strip + ds) // planes != g)
+                valid, dev = (g + ds >= 0) & (g + ds < gys), {"build": z, "gx": y, "gy": g + ds}
+            else:
+                valid, dev = near(ds, dy), owner(strip + ds, y + dy)
 
             @pl.when(valid)
             def _():
-                pl.semaphore_signal(barrier, inc=1, device_id=owner(strip + ds, y + dy), device_id_type=MESH)
+                pl.semaphore_signal(barrier, inc=1, device_id=dev, device_id_type=MESH)
 
             count += jnp.where(valid, 1, 0)
+    for ds in (-1, 1):
+        valid = (g + ds >= 0) & (g + ds < gys)
+        dev = owner(strip - k + (planes if ds == 1 else -1), y)
+
+        @pl.when(valid & (dev["build"] != z))
+        def _():
+            pl.semaphore_signal(barrier, inc=1, device_id=dev, device_id_type=MESH)
+
+        count += jnp.where(valid & (k == (planes - 1 if ds == 1 else 0)), planes - 1, 0)
 
     lane = lax.broadcasted_iota(jnp.int32, (REGION, LANES), 1)
     row = jnp.where(lane < 96, lane, lane - LANES) + y * ROWS
@@ -108,15 +121,15 @@
         wait(raw.at[which], raw_sem.at[which])
         for n in range(OWN // 2):
             both = jnp.concatenate([raw[which, 2 * n], raw[which, 2 * n + 1]], axis=0)
-            nat[which, n] = both.T
+            nat[which, n, EDGE : EDGE + width] = both.T
 
     transpose_in(DESIGN)
     pl.semaphore_wait(barrier, count)
 
     def swap(which, go):
         def step(i, _):
-            p = (z + i) % planes
-            src = nat.at[which, :, pl.ds(pl.multiple_of(flip(g, p) * STRIP, STRIP), STRIP)]
+            p = (z + planes // 2 + (1 - 2 * (i % 2)) * ((i + 1) // 2) + planes) % planes
+            src = nat.at[which, :, pl.ds(pl.multiple_of(EDGE + flip(g, p) * STRIP, 8), STRIP)]
             dst = ext.at[which, pl.ds(2 * z, 2), pl.ds(STRIP, STRIP)]
 
             @pl.when(p != z)
@@ -140,42 +153,6 @@
         for i in range(per_segment):
             p = per_segment * seg + i
             wait(ext.at[which, pl.ds(2 * p, 2), pl.ds(STRIP, STRIP)], swap_r.at[which, p])
-
-    def result(which, seg, go):
-        def step(i, _):
-            p = per_segment * seg + i
-            src = results.at[which, pl.ds(2 * p, 2)]
-            dst = home.at[which, :, pl.ds(pl.multiple_of(k * STRIP, STRIP), STRIP)]
-
-            @pl.when(p != z)
-            def _():
-                if go:
-                    start(src, dst, out_s.at[which, p], out_r.at[which, k], {"build": p, "gx": y, "gy": g})
-                else:
-                    wait(src, out_s.at[which, p])
-
-            if go:
-
-                @pl.when(p == z)
-                def _():
-                    pltpu.make_async_copy(src, dst, out_r.at[which, k]).start()
-
-            return 0
-
-        lax.fori_loop(0, per_segment, step, 0)
-
-    def result_land(which):
-        def step(n, _):
-            there = pl.ds(pl.multiple_of(n * STRIP, STRIP), STRIP)
-            wait(home.at[which, :, there], out_r.at[which, n])
-            return 0
-
-        lax.fori_loop(0, planes, step, 0)
-        out = (pr_ref, gr_ref)[which]
-        for n in range(OWN // 2):
-            both = home[which, n].T
-            out[2 * n] = both[0:ROWS]
-            out[2 * n + 1] = both[ROWS:]
 
     def parts(which):
         if which == COTANGENT:
@@ -212,36 +189,50 @@
                 def _():
                     wait(ext.at[which, pairs, there], col_r.at[which, seg, n, side])
 
+    def direct(which, seg):
+        return (which, seg) in ((WEIGHT, last), *((DESIGN, n) for n in range(2)))
+
+    def spread(which, seg, ds):
+        if direct(which, seg):
+            return pl.ds(STRIP, STRIP), pl.ds((1 - ds) * STRIP, STRIP)
+        return pl.ds(0, REGION), pl.ds(0, REGION)
+
     def bands(which, seg, go):
+        lo, hi = (STRIP, 2 * STRIP) if direct(which, seg) else (0, REGION)
         if go:
             for quad in range(2):
                 for side in range(2):
                     packed = None
                     for m in range(4):
-                        value = turned(ext[which, PAIRS * seg + 4 * quad + m], 16 * m)
+                        value = turned(ext[which, PAIRS * seg + 4 * quad + m, lo:hi], 16 * m)
                         if packed is None:
                             packed = value
                         else:
-                            slot = (lane + (16 if side == 0 else 64) - 16 * m) % 64
+                            slot = (lane[lo:hi] + (80 if side == 0 else 64) - 16 * m) % 64
                             packed = jnp.where(slot < 16, value, packed)
-                    band_out[which, side, 2 * seg + quad] = packed
+                    band_out[which, side, 2 * seg + quad, lo:hi] = packed
         for side, dy in ((0, 1), (1, -1)):
-            src = band_out.at[which, side, pl.ds(2 * seg, 2)]
-            dst = band_in.at[which, side, pl.ds(2 * seg, 2)]
-
-            @pl.when(near(0, dy))
-            def _():
-                if go:
-                    start(src, dst, band_s.at[which, seg, side], band_r.at[which, seg, side], owner(strip, y + dy))
-                else:
-                    wait(src, band_s.at[which, seg, side])
+            for ds in (-1, 1, 0) if direct(which, seg) else (0,):
+                here, there = spread(which, seg, ds)
+                src = band_out.at[which, side, pl.ds(2 * seg, 2), here]
+                dst = band_in.at[which, side, pl.ds(2 * seg, 2), there]
+
+                @pl.when(near(ds, dy))
+                def _():
+                    if go:
+                        start(src, dst, band_s.at[which, seg, side, 1 - ds], band_r.at[which, seg, side, 1 - ds],
+                              owner(strip + ds, y + dy))
+                    else:
+                        wait(src, band_s.at[which, seg, side, 1 - ds])
 
     def bands_land(which, seg):
         for side, dy in ((0, -1), (1, 1)):
-
-            @pl.when(near(0, dy))
-            def _():
-                wait(band_in.at[which, side, pl.ds(2 * seg, 2)], band_r.at[which, seg, side])
+            for ds in (-1, 1, 0) if direct(which, seg) else (0,):
+                _, there = spread(which, seg, ds)
+
+                @pl.when(near(-ds, dy))
+                def _():
+                    wait(band_in.at[which, side, pl.ds(2 * seg, 2), there], band_r.at[which, seg, side, 1 - ds])
 
     def field(which, pair, m, odd, lo, hi):
         lanes = lane[lo:hi]
@@ -258,19 +249,16 @@
         return jnp.where(lane_own < 64, even, turned(odd, 64))
 
     def sync(n, go):
-        for ds in (-1, 0, 1):
-            for dy in (-1, 0, 1):
-                if ds == 0 and dy == 0:
-                    continue
-                src, dst = sync_out.at[n], sync_in.at[n, 1 - dy, pl.ds((1 - ds) * STRIP, STRIP)]
-
-                @pl.when(near(ds, dy))
-                def _():
-                    if go:
-                        start(src, dst, sync_s.at[n, 1 - dy, 1 - ds], sync_r.at[n, 1 - dy, 1 - ds],
-                              owner(strip + ds, y + dy))
-                    else:
-                        wait(src, sync_s.at[n, 1 - dy, 1 - ds])
+        for ds, dy in ((-1, -1), (-1, 1), (1, -1), (1, 1), (-1, 0), (1, 0), (0, -1), (0, 1)):
+            src, dst = sync_out.at[n], sync_in.at[n, 1 - dy, pl.ds((1 - ds) * STRIP, STRIP)]
+
+            @pl.when(near(ds, dy))
+            def _():
+                if go:
+                    start(src, dst, sync_s.at[n, 1 - dy, 1 - ds], sync_r.at[n, 1 - dy, 1 - ds],
+                          owner(strip + ds, y + dy))
+                else:
+                    wait(src, sync_s.at[n, 1 - dy, 1 - ds])
 
     def give(n, value):
         sync_out[n] = value
@@ -312,13 +300,15 @@
                 pair = PAIRS * seg + 2 * quad + i
                 layer = 2 * pair + odd
                 des = field_dynamic(DESIGN, pair, quad, m, odd, lo, hi)
-                bound, excess, under, inverse = terms(five(w), des)
-                fresh = 0.5 * (des + bound - under * inverse + SOFT_ROOT)
-                w = jnp.where(mask, jnp.exp2(fresh * (SHARPNESS * LOG2_E)), 1.0)
+                level = jnp.log2(five(w))
+                excess = (des + math.log(5.0) / SHARPNESS) - level * (1.0 / (LOG2_E * SHARPNESS))
+                under = excess * excess + SOFTNESS
+                start_of = des * HALF + (SOFT_ROOT - math.log(5.0) / SHARPNESS) * HALF
+                power = (start_of + 0.5 * level) - under * lax.rsqrt(under) * HALF
+                w = jnp.where(mask, jnp.exp2(power), 1.0)
                 weights[layer + 1, lo:hi] = w
-                saved.append((own_of(w, lo), own_of(fresh, lo)))
-            ext[WEIGHT, pair, STRIP : 2 * STRIP] = paired(saved[0][0], saved[1][0])
-            results[0, pair] = paired(saved[0][1], saved[1][1])
+                saved.append(own_of(w, lo))
+            ext[WEIGHT, pair, STRIP : 2 * STRIP] = paired(*saved)
         return w
 
     def field_dynamic(which, pair, part, i, odd, lo, hi):
@@ -336,6 +326,8 @@
         bands_land(WEIGHT, seg)
         for n in range(3, PAIRS):
             for odd in range(2):
+                if n == PAIRS - 1 and odd and seg < last:
+                    continue
                 value = field(WEIGHT, PAIRS * seg + n, n % 4, odd, 0, REGION)
                 weights[DEPTH * seg + 2 * n + odd + 1] = jnp.where(inside_ref[...] > 0.5, value, 1.0)
 
@@ -347,34 +339,213 @@
             bound, excess, under, inverse = terms(total, field(DESIGN, pair, (j // 2) % 4, j % 2, lo, hi))
             ratio = excess * inverse
             a1[layer, lo:hi] = jnp.where(inside_ref[lo:hi] > 0.5, 0.5 * (1.0 + ratio) / total, 0.0)
-            a2[layer] = own_of(0.5 * (1.0 - ratio), lo)
 
     def backward_segment(seg, q):
-        saved = None
-        for j in range(DEPTH - 1, -1, -1):
+        for j in range(DEPTH - 1, OWN - 1 if seg == 0 else -1, -1):
             lo, hi = narrow if j < DEPTH // 2 else wide
             if j == DEPTH // 2 - 1:
                 q = q[half : REGION - half]
             layer, pair = DEPTH * seg + j, PAIRS * seg + j // 2
             adjoint = field(COTANGENT, pair, (j // 2) % 4, j % 2, lo, hi) + weights[layer + 1, lo:hi] * five(q)
             q = jnp.where(inside_ref[lo:hi] > 0.5, adjoint * a1[layer, lo:hi], 0.0)
-            slope = own_of(adjoint, lo) * a2[layer]
+            if j % OWN == 0 and j > 0:
+                pullbacks[layer // OWN - 1] = own_of(q, lo)
+        return own_of(q, half)
+
+    on_right = k > 0
+    onward = jnp.where(on_right, g + 1, g - 1)
+    outermost = ((k == 0) & (g > 0)) | ((k == planes - 1) & (g < gys - 1))
+
+    def piece(kind, p, go):
+        def source(first, number):
+            first = pl.multiple_of(first, 8)
+            if kind == 0:
+                return weights.at[OWN * p, pl.ds(pl.multiple_of(STRIP + first, 8), number)]
+            return pullbacks.at[p, pl.ds(first, number)]
+
+        src = source(0, STRIP)
+        dst = border.at[kind, pl.ds(pl.multiple_of(EDGE + k * STRIP, 8), STRIP)]
+
+        @pl.when(p != z)
+        def _():
+            if go:
+                start(src, dst, border_s.at[kind, p], border_r.at[kind, k], {"build": p, "gx": y, "gy": g})
+            else:
+                wait(src, border_s.at[kind, p])
+
+        if go:
+
+            @pl.when(p == z)
+            def _():
+                pltpu.make_async_copy(src, dst, border_r.at[kind, k]).start()
+
+        rim = source(jnp.where(on_right, STRIP - EDGE, 0), EDGE)
+        there = border.at[kind, pl.ds(pl.multiple_of(jnp.where(on_right, 0, EDGE + width), 8), EDGE)]
+
+        @pl.when(outermost)
+        def _():
+            if go:
+                start(rim, there, rim_s.at[kind, p], rim_r.at[kind, jnp.where(on_right, 0, 1)],
+                      {"build": p, "gx": y, "gy": onward})
+            else:
+                wait(rim, rim_s.at[kind, p])
+
+    def lift(seg):
+        for p in range(per_segment * seg, min(per_segment * (seg + 1), planes - 1)):
+            piece(1, p, True)
+
+    def support(seg):
+        for p in range(max(1, per_segment * seg), per_segment * (seg + 1)):
+            piece(0, p, True)
+
+    def present(kind):
+        return z > 0 if kind == 0 else z < planes - 1
+
+    def border_land(kind):
+        @pl.when(present(kind))
+        def _():
+            def step(n, _):
+                wait(border.at[kind, pl.ds(pl.multiple_of(EDGE + n * STRIP, 8), STRIP)], border_r.at[kind, n])
+                return 0
+
+            lax.fori_loop(0, planes, step, 0)
+
+        for side, there, valid in ((0, 0, g > 0), (1, EDGE + width, g < gys - 1)):
+
+            @pl.when(valid & present(kind))
+            def _():
+                wait(border.at[kind, pl.ds(there, EDGE)], rim_r.at[kind, side])
+
+    def beside(side):
+        dg = 1 - 2 * side
+        here = pl.ds(width, EDGE) if side == 0 else pl.ds(EDGE, EDGE)
+        there = pl.ds(0, EDGE) if side == 0 else pl.ds(EDGE + width, EDGE)
+        return here, there, (g + dg >= 0) & (g + dg < gys), {"build": z, "gx": y, "gy": g + dg}
+
+    def sides(which, go):
+        for side in range(2):
+            here, there, valid, dev = beside(side)
+            src, dst = nat.at[which, :, here], nat.at[which, :, there]
+
+            @pl.when(valid)
+            def _():
+                if go:
+                    start(src, dst, side_s.at[which, side], side_r.at[which, side], dev)
+                else:
+                    wait(src, side_s.at[which, side])
+
+    def sides_land(which):
+        for side in range(2):
+            _, there, _, _ = beside(side)
+            _, _, valid, _ = beside(1 - side)
+
+            @pl.when(valid)
+            def _():
+                wait(nat.at[which, :, there], side_r.at[which, side])
+
+    lane_nat = lax.broadcasted_iota(jnp.int32, (width + 2 * EDGE, LANES), 1)
+
+    def rows(go):
+        for side, dy in ((0, 1), (1, -1)):
+            if go:
+                packed = nat[DESIGN, 0]
+                for m in range(1, OWN):
+                    slot = (lane_nat + (80 if side == 0 else 64) - 16 * m) % 64
+                    packed = jnp.where(slot < 16, turned(nat[m // 2, m % 2], 16 * m), packed)
+                nat_out[side] = packed
+
+            @pl.when((y + dy >= 0) & (y + dy < xs))
+            def _():
+                dev = {"build": z, "gx": y + dy, "gy": g}
+                if go:
+                    start(nat_out.at[side], nat_in.at[side], row_s.at[side], row_r.at[side], dev)
+                else:
+                    wait(nat_out.at[side], row_s.at[side])
+
+    def rows_land():
+        for side, dy in ((0, -1), (1, 1)):
+
+            @pl.when((y + dy >= 0) & (y + dy < xs))
+            def _():
+                wait(nat_in.at[side], row_r.at[side])
+
+    reach = CHUNK + 2 * EDGE
+    lane_reach = lax.broadcasted_iota(jnp.int32, (reach, LANES), 1)
+
+    def own_field(which, j, span):
+        own = nat[which, j // 2, span]
+        shift = -16 * (2 * which + j // 2) + (0 if j % 2 else 64)
+        above = turned(nat_in[0, span], shift)
+        below = turned(nat_in[1, span], shift)
+        own = turned(own, 64) if j % 2 else own
+        return jnp.where(lane_reach < 64, own, jnp.where(lane_reach < 96, below, above))
+
+    def chunk_mask(c):
+        at_row = jnp.where(lane_reach < 96, lane_reach, lane_reach - LANES) + y * ROWS
+        at_col = lax.broadcasted_iota(jnp.int32, (reach, LANES), 0) + (width * g + CHUNK * c - EDGE)
+        return (at_row >= 0) & (at_row < xs * ROWS) & (at_col >= 0) & (at_col < gys * width)
+
+    def both_layers(even, odd):
+        return jnp.where(lane_reach[0:CHUNK] < 64, even, turned(odd, 64))
+
+    def own_forward(c, _):
+        span = pl.ds(pl.multiple_of(CHUNK * c, CHUNK), reach)
+        mask = chunk_mask(c)
+        w = jnp.where(z == 0, math.exp(SHARPNESS), border[0, span])
+        w = jnp.where(mask, w, 1.0)
+        saved = None
+        for j in range(OWN):
+            des = own_field(DESIGN, j, span)
+            total = five(w)
+            bound, excess, under, inverse = terms(total, des)
+            ratio = excess * inverse
+            na1[c, j] = jnp.where(mask, 0.5 * (1.0 + ratio) / total, 0.0)
+            na2[c, j] = 0.5 * (1.0 - ratio[EDGE : EDGE + CHUNK])
+            fresh = 0.5 * (des + bound - under * inverse + SOFT_ROOT)
+            w = jnp.where(mask, jnp.exp2(fresh * (SHARPNESS * LOG2_E)), 1.0)
+            nw[c, j] = w
+            mine = fresh[EDGE : EDGE + CHUNK]
             if j % 2:
-                saved = slope
-            else:
-                results[1, pair] = paired(slope, saved)
-        return own_of(q, half)
-
-    last = segments - 1
+                home[0, j // 2, pl.ds(pl.multiple_of(CHUNK * c, CHUNK), CHUNK)] = both_layers(saved, mine)
+            saved = mine
+        return 0
+
+    def own_backward(c, _):
+        span = pl.ds(pl.multiple_of(CHUNK * c, CHUNK), reach)
+        mask = chunk_mask(c)
+        q = jnp.where(mask & present(1), border[1, span], 0.0)
+        saved = None
+        for j in range(OWN - 1, -1, -1):
+            adjoint = own_field(COTANGENT, j, span) + nw[c, j] * five(q)
+            q = jnp.where(mask, adjoint * na1[c, j], 0.0)
+            mine = adjoint[EDGE : EDGE + CHUNK] * na2[c, j]
+            if j % 2 == 0:
+                home[1, j // 2, pl.ds(pl.multiple_of(CHUNK * c, CHUNK), CHUNK)] = both_layers(mine, saved)
+            saved = mine
+        return 0
+
+    def put(which):
+        out = (pr_ref, gr_ref)[which]
+        for n in range(OWN // 2):
+            both = home[which, n].T
+            out[2 * n] = both[0:ROWS]
+            out[2 * n + 1] = both[ROWS:]
+
     swap(DESIGN, True)
     transpose_in(COTANGENT)
+    for which in (DESIGN, COTANGENT):
+        sides(which, True)
+    for which in (DESIGN, COTANGENT):
+        sides_land(which)
+    rows(True)
     swap_land(DESIGN, 0)
+    bands(DESIGN, 0, True)
     columns(DESIGN, 0, True)
-    columns_land(DESIGN, 0)
-    bands(DESIGN, 0, True)
     swap(COTANGENT, True)
     if last > 0:
         swap_land(DESIGN, 1)
+        if direct(DESIGN, 1):
+            bands(DESIGN, 1, True)
         columns(DESIGN, 1, True)
     for seg in range(segments):
         if seg == 0:
@@ -382,35 +553,50 @@
         else:
             w = taken(seg - 1, 1.0)
         weights[DEPTH * seg] = w
+        if direct(DESIGN, seg):
+            columns_land(DESIGN, seg)
         bands_land(DESIGN, seg)
         w = forward_segment(seg, w)
         if seg < last:
             give(seg, w)
+        if seg == last:
+            bands(WEIGHT, seg, True)
         columns(WEIGHT, seg, True)
-        result(0, seg, True)
         if seg < last:
-            columns_land(DESIGN, seg + 1)
-            bands(DESIGN, seg + 1, True)
+            if not direct(DESIGN, seg + 1):
+                columns_land(DESIGN, seg + 1)
+                bands(DESIGN, seg + 1, True)
         if seg + 1 < last:
             swap_land(DESIGN, seg + 2)
+            if direct(DESIGN, seg + 2):
+                bands(DESIGN, seg + 2, True)
             columns(DESIGN, seg + 2, True)
         if seg > 0:
             columns_land(WEIGHT, seg - 1)
             bands(WEIGHT, seg - 1, True)
-        if seg == last - 1:
+        if seg > 1:
+            fill(seg - 2)
+            support(seg - 2)
+        if seg == max(0, last - 2):
             swap_land(COTANGENT, last)
             columns(COTANGENT, last, True)
-
-    if last == 0:
-        swap_land(COTANGENT, last)
-        columns(COTANGENT, last, True)
+        if seg == max(0, last - 1):
+            columns_land(COTANGENT, last)
+            bands(COTANGENT, last, True)
+            if last > 0:
+                swap_land(COTANGENT, last - 1)
+                columns(COTANGENT, last - 1, True)
+
+    if last > 0:
+        columns_land(COTANGENT, last - 1)
+        bands(COTANGENT, last - 1, True)
+    if last > 1:
+        swap_land(COTANGENT, last - 2)
+        columns(COTANGENT, last - 2, True)
+    if last > 0:
+        fill(last - 1)
+        prepare(last - 1)
     columns_land(WEIGHT, last)
-    bands(WEIGHT, last, True)
-    columns_land(COTANGENT, last)
-    bands(COTANGENT, last, True)
-    if last > 0:
-        swap_land(COTANGENT, last - 1)
-        columns(COTANGENT, last - 1, True)
     fill(last)
     prepare(last)
     for seg in range(last, -1, -1):
@@ -418,33 +604,48 @@
             q = jnp.zeros((REGION, LANES), jnp.float32)
         else:
             q = taken(last + last - 1 - seg, 0.0)
+            pullbacks[per_segment * (seg + 1) - 1] = own_of(q, 0)
         bands_land(COTANGENT, seg)
         q = backward_segment(seg, q)
         if seg > 0:
             give(last + last - seg, q)
-        result(1, seg, True)
-        if seg > 0:
-            columns_land(COTANGENT, seg - 1)
-            bands(COTANGENT, seg - 1, True)
-            fill(seg - 1)
-            prepare(seg - 1)
+        lift(seg)
         if seg > 1:
-            swap_land(COTANGENT, seg - 2)
-            columns(COTANGENT, seg - 2, True)
-        if seg == min(1, last):
-            result_land(0)
+            columns_land(COTANGENT, seg - 2)
+            bands(COTANGENT, seg - 2, True)
+        if seg > 2:
+            swap_land(COTANGENT, seg - 3)
+            columns(COTANGENT, seg - 3, True)
+        if seg > 1:
+            prepare(seg - 2)
+        if seg == last:
+            for other in range(max(0, last - 1), last + 1):
+                support(other)
+    rows_land()
+    border_land(0)
+    lax.fori_loop(0, width // CHUNK, own_forward, 0)
+    put(0)
 
     for which in (DESIGN, COTANGENT):
         swap(which, False)
+        sides(which, False)
     for seg in range(segments):
         for which in (DESIGN, COTANGENT, WEIGHT):
             columns(which, seg, False)
             bands(which, seg, False)
-        for which in range(2):
-            result(which, seg, False)
     for n in range(2 * last):
         sync(n, False)
-    result_land(1)
+    rows(False)
+    for p in range(1, planes):
+        piece(0, p, False)
+    for p in range(per_segment, planes - 1):
+        piece(1, p, False)
+
+    border_land(1)
+    lax.fori_loop(0, width // CHUNK, own_backward, 0)
+    put(1)
+    for p in range(min(per_segment, planes - 1)):
+        piece(1, p, False)
 
 
 def local(design, cotangent):
@@ -452,6 +653,8 @@
     planes = lax.axis_size("build")
     layers = planes * OWN
     segments = layers // DEPTH
+    width = planes * STRIP
+    chunks = width // CHUNK
     syncs = max(1, 2 * (segments - 1))
     f32 = lambda *shape: pltpu.VMEM(shape, jnp.float32)
     dma = lambda *shape: pltpu.SemaphoreType.DMA(shape)
@@ -463,30 +666,41 @@
         in_specs=[anywhere, anywhere],
         out_specs=(vmem, vmem),
         scratch_shapes=[
-            f32(2, OWN, ROWS, planes * STRIP),
-            f32(2, OWN // 2, planes * STRIP, LANES),
+            f32(2, OWN, ROWS, width),
+            f32(2, OWN // 2, width + 2 * EDGE, LANES),
             f32(3, layers // 2, REGION, LANES),
             f32(3, 2, layers // 8, REGION, LANES),
             f32(3, 2, layers // 8, REGION, LANES),
             f32(layers + 1, REGION, LANES),
             f32(layers, REGION, LANES),
-            f32(layers, STRIP, LANES),
-            f32(2, layers // 2, STRIP, LANES),
-            f32(2, OWN // 2, planes * STRIP, LANES),
             f32(syncs, STRIP, LANES),
             f32(syncs, 3, REGION, LANES),
             f32(REGION, LANES),
+            f32(2, width + 2 * EDGE, LANES),
+            f32(2, width + 2 * EDGE, LANES),
+            f32(2, width + 2 * EDGE, LANES),
+            f32(planes, STRIP, LANES),
+            f32(chunks, OWN, CHUNK + 2 * EDGE, LANES),
+            f32(chunks, OWN, CHUNK + 2 * EDGE, LANES),
+            f32(chunks, OWN, CHUNK, LANES),
+            f32(2, OWN // 2, width, LANES),
             dma(2),
             dma(2, planes),
             dma(2, planes),
             dma(3, segments, 2, 2),
             dma(3, segments, 2, 2),
-            dma(3, segments, 2),
-            dma(3, segments, 2),
+            dma(3, segments, 2, 3),
+            dma(3, segments, 2, 3),
             dma(syncs, 3, 3),
             dma(syncs, 3, 3),
+            dma(2, 2),
+            dma(2, 2),
+            dma(2),
+            dma(2),
             dma(2, planes),
             dma(2, planes),
+            dma(2, planes),
+            dma(2, 2),
         ],
         compiler_params=pltpu.CompilerParams(
             collective_id=0, has_side_effects=True, vmem_limit_bytes=40 * 1024 * 1024

time: 114 us -> 103 us (0.904)
  Pallas kernels: 110 us -> 98.9 us
    pallas_call x1, Pallas kernels: 110 us -> 98.9 us  [local(): pl.pallas_call(kernel, out_shape=(shard, shard), in_specs=[anywhere, anyw...]
where the time goes in v3:
time: 103 us
  Pallas kernels  98.9 us (96%)
  local copies, waits for them, and re-layouts  3.3 us (3%)
    pallas_call x1, Pallas kernels, local(): pl.pallas_call(kernel, out_shape=(shard, shard), in_specs=[anywhere, anyw...  98.9 us
    unnamed x6, local copies, waits for them, and re-layouts  3.3 us

profile of v3, /device:TPU:8, one launch (start us, length us, event | category | flops | bytes accessed | tf_op | source)
XLA Modules:
  0.0 102.8 jit_solution(15305916667024295628)
XLA Ops:
  0.6 0.0 copy-start
  0.6 0.9 copy-done
  1.6 0.0 copy-start.1
  1.6 0.9 copy-done.1
  2.5 98.9 %shard_map.41 = (f32[4,64,256]{2,1,0:T(8,128)S(1)}, f32[4,64,256]{2,1,0:T(8,128)S(1)}) custom-call(f32[4,64,256]{2,1,0:T(8,128)S(1)} %copy-done, f32[4,64,256]{2,1,0:T(8,128)S(1)} %copy-done.1), custom_call_target="tpu_custom_call" | custom-call | tf_op jit(solution)/shard_map/pallas_call | solution.py:663
  101.4 0.7 copy.6
  102.1 0.7 copy.7
Async XLA Ops:
  0.6 1.0 copy-start
  1.6 0.9 copy-start.1

commit v4 on v3

--- a/solution.py
+++ b/solution.py
@@ -541,12 +541,12 @@
     swap_land(DESIGN, 0)
     bands(DESIGN, 0, True)
     columns(DESIGN, 0, True)
-    swap(COTANGENT, True)
     if last > 0:
         swap_land(DESIGN, 1)
         if direct(DESIGN, 1):
             bands(DESIGN, 1, True)
         columns(DESIGN, 1, True)
+    swap(COTANGENT, True)
     for seg in range(segments):
         if seg == 0:
             w = jnp.where(inside_ref[...] > 0.5, math.exp(SHARPNESS), 1.0)
@@ -618,7 +618,7 @@
             columns(COTANGENT, seg - 3, True)
         if seg > 1:
             prepare(seg - 2)
-        if seg == last:
+        if seg == max(0, last - 1):
             for other in range(max(0, last - 1), last + 1):
                 support(other)
     rows_land()

time: 103 us -> 102 us (level)
  the two profiles are of different devices: /device:TPU:8 before, /device:TPU:12 now
where the time goes in v4:
time: 102 us
  Pallas kernels  98.3 us (96%)
  local copies, waits for them, and re-layouts  3.3 us (3%)
    pallas_call x1, Pallas kernels, local(): pl.pallas_call(kernel, out_shape=(shard, shard), in_specs=[anywhere, anyw...  98.3 us
    unnamed x6, local copies, waits for them, and re-layouts  3.3 us

profile of v4, /device:TPU:12, one launch (start us, length us, event | category | flops | bytes accessed | tf_op | source)
XLA Modules:
  0.0 102.3 jit_solution(1791427076891501536)
XLA Ops:
  0.6 0.0 copy-start
  0.6 0.9 copy-done
  1.6 0.0 copy-start.1
  1.6 0.9 copy-done.1
  2.5 98.3 %shard_map.41 = (f32[4,64,256]{2,1,0:T(8,128)S(1)}, f32[4,64,256]{2,1,0:T(8,128)S(1)}) custom-call(f32[4,64,256]{2,1,0:T(8,128)S(1)} %copy-done, f32[4,64,256]{2,1,0:T(8,128)S(1)} %copy-done.1), custom_call_target="tpu_custom_call" | custom-call | tf_op jit(solution)/shard_map/pallas_call | solution.py:663
  100.9 0.7 copy.6
  101.6 0.7 copy.7
Async XLA Ops:
  0.6 1.0 copy-start
  1.6 0.9 copy-start.1
